TPU v7x, 32 devices: a whole 2x2x4 slice. The times are simulated.
32 devices in a mesh: mode: 4 (over z), rows: 8 (over y, x, core).
Axes of the slice: x: 2, y: 2, z: 4, core: 2. Of those that a mesh axis runs over, the one named last changes fastest.
Arguments:
- object_real: float32 [8, 2048, 2048], P('mode', 'rows'), may hold values from -6 to 6
- object_imag: float32 [8, 2048, 2048], P('mode', 'rows'), may hold values from -6 to 6
- pupil_real: float32 [1024, 1024], P('rows'), may hold values from -0.7 to 0.7
- pupil_imag: float32 [1024, 1024], P('rows'), may hold values from -0.7 to 0.7
- measured: float32 [1, 1024, 1024], P(None, 'rows'), may hold values from 1 to 5
- source_mask: int32 [1, 3], replicated, may hold values from 0 to 1, as said below
- offsets: int32 [3, 2], replicated, may hold values from 0 to 1024
Outputs:
- updated_real: float32 [8, 2048, 2048], P('mode', 'rows')
- updated_imag: float32 [8, 2048, 2048], P('mode', 'rows')
Inputs may be any that keep to these rules, and one draw needn't show every extreme that they name: `source_mask`: every frame has at least one LED lit and at least one dark.
All inputs are finite; a program needn't handle non-finite values.
Results may differ from a plain program's by a relative error of at most 0.0003.
Values sent between devices are 32-bit elements; how exact they have to be, the bound alone decides.
No kernel may reach another device: no remote copies, remote signals or barrier semaphores. Data moves between devices by JAX's collectives and lax.ppermute only.
A program may use at most 128 MiB of HBM per device.

v0:
```python
import functools
import math

import jax
import jax.numpy as jnp
import ml_dtypes
import numpy as np
from jax import lax
from jax.experimental import pallas as pl
from jax.experimental.pallas import tpu as pltpu
from jax.sharding import PartitionSpec as P

FLOOR_TERM = 0.5
HIGHEST_PREC = lax.Precision.HIGHEST


def dft_tables(length):
    indices = jnp.arange(length, dtype=jnp.int32)
    phases = indices[:, None] * indices[None, :] % length
    angles = phases.astype(jnp.float32) * (2.0 * math.pi / length)
    scale_factor = 1.0 / math.sqrt(length)
    cos_table = jnp.cos(angles) * scale_factor
    sin_table = jnp.sin(angles) * scale_factor
    return (
        jnp.concatenate([cos_table, sin_table], axis=1),
        jnp.concatenate([cos_table, sin_table], axis=0),
    )


def transform(form, table, real_part, imag_part, axis, direction_sign):
    result = jnp.einsum(form, jnp.stack([real_part, imag_part]), table, precision=HIGHEST_PREC)
    length = result.shape[axis] // 2
    with_cos = lax.slice_in_dim(result, 0, length, axis=axis)
    with_sin = lax.slice_in_dim(result, length, 2 * length, axis=axis)
    return (with_cos[0] - direction_sign * with_sin[1], with_cos[1] + direction_sign * with_sin[0])


def right_product(real_part, imag_part, wide_cols, direction_sign):
    return transform("smlck,kj->smlcj", wide_cols, real_part, imag_part, 4, direction_sign)


def forward_fields(
    part_real, part_imag, pupil_real, pupil_imag, offsets, wide_cols, wide_rows, length
):
    source_count = offsets.shape[0]
    groups = lax.axis_size("rows")
    crop_real = jnp.stack(
        [
            lax.dynamic_slice_in_dim(part_real, offsets[source_index, 1], length, 2)
            for source_index in range(source_count)
        ],
        axis=1,
    )
    crop_imag = jnp.stack(
        [
            lax.dynamic_slice_in_dim(part_imag, offsets[source_index, 1], length, 2)
            for source_index in range(source_count)
        ],
        axis=1,
    )
    got_real, got_imag = (
        lax.all_to_all(
            jnp.swapaxes(crop_real, 2, 3), "rows", split_axis=2, concat_axis=3, tiled=True
        ),
        lax.all_to_all(
            jnp.swapaxes(crop_imag, 2, 3), "rows", split_axis=2, concat_axis=3, tiled=True
        ),
    )
    win_real = jnp.stack(
        [
            lax.dynamic_slice_in_dim(got_real[:, source_index], offsets[source_index, 0], length, 2)
            for source_index in range(source_count)
        ],
        axis=1,
    )
    win_imag = jnp.stack(
        [
            lax.dynamic_slice_in_dim(got_imag[:, source_index], offsets[source_index, 0], length, 2)
            for source_index in range(source_count)
        ],
        axis=1,
    )
    lifted_real = pupil_real * win_real - pupil_imag * win_imag
    lifted_imag = pupil_real * win_imag + pupil_imag * win_real
    half_real, half_imag = transform("smlcr,yr->smlyc", wide_rows, lifted_real, lifted_imag, 3, 1.0)
    layout = half_real.shape
    blocked = (layout[0], layout[1], groups, layout[2] // groups, layout[3])
    back_real, back_imag = (
        lax.all_to_all(half_real.reshape(blocked), "rows", split_axis=2, concat_axis=4, tiled=True),
        lax.all_to_all(half_imag.reshape(blocked), "rows", split_axis=2, concat_axis=4, tiled=True),
    )
    flat = (layout[0], layout[1], layout[2] // groups, layout[3] * groups)
    return right_product(back_real.reshape(flat), back_imag.reshape(flat), wide_cols, 1.0)


def spectral_updates(diff_real, diff_imag, pupil_real, pupil_imag, offsets, wide_cols, size_k):
    source_count = offsets.shape[0]
    groups = lax.axis_size("rows")
    col_real, col_imag = right_product(diff_real, diff_imag, wide_cols, -1.0)
    layout = col_real.shape
    blocked = (layout[0], layout[1], layout[2], groups, layout[3] // groups)
    got_real, got_imag = (
        lax.all_to_all(col_real.reshape(blocked), "rows", split_axis=3, concat_axis=2, tiled=True),
        lax.all_to_all(col_imag.reshape(blocked), "rows", split_axis=3, concat_axis=2, tiled=True),
    )
    flat = (layout[0], layout[1], layout[2] * groups, layout[3] // groups)
    full_real = got_real.reshape(flat)
    full_imag = got_imag.reshape(flat)
    delta_real, delta_imag = transform("smlyc,yk->smlck", wide_cols, full_real, full_imag, 4, -1.0)
    upd_real = pupil_real * delta_real + pupil_imag * delta_imag
    upd_imag = pupil_real * delta_imag - pupil_imag * delta_real
    blank = jnp.zeros((layout[0], layout[3] // groups, size_k), jnp.float32)
    placed_real = jnp.stack(
        [
            lax.dynamic_update_slice_in_dim(
                blank, upd_real[:, source_index], offsets[source_index, 0], 2
            )
            for source_index in range(source_count)
        ],
        axis=1,
    )
    placed_imag = jnp.stack(
        [
            lax.dynamic_update_slice_in_dim(
                blank, upd_imag[:, source_index], offsets[source_index, 0], 2
            )
            for source_index in range(source_count)
        ],
        axis=1,
    )
    return (
        lax.all_to_all(placed_real, "rows", split_axis=3, concat_axis=2, tiled=True),
        lax.all_to_all(placed_imag, "rows", split_axis=3, concat_axis=2, tiled=True),
    )


def add_window(target, incoming, start_col, length):
    current = lax.dynamic_slice_in_dim(target, start_col, length, 2)
    return lax.dynamic_update_slice_in_dim(
        target, current + jnp.swapaxes(incoming, 1, 2), start_col, 2
    )


def body(object_real, object_imag, pupil_real, pupil_imag, measured, source_mask, offsets):
    length = pupil_real.shape[1]
    size_k = object_real.shape[2]
    source_count = offsets.shape[0]
    wide_cols, wide_rows = dft_tables(length)
    spec_real, spec_imag = (object_real, object_imag)
    weights = source_mask[0].astype(jnp.float32)
    field_real, field_imag = forward_fields(
        spec_real, spec_imag, pupil_real, pupil_imag, offsets, wide_cols, wide_rows, length
    )
    powers = jnp.sum(field_real * field_real + field_imag * field_imag, axis=0)
    partial_sum = jnp.tensordot(weights, powers, axes=1)
    share = lax.psum_scatter(partial_sum, "mode", scatter_dimension=0, tiled=True)
    share_rows = share.shape[0]
    measured_share = lax.dynamic_slice_in_dim(
        measured[0], lax.axis_index("mode") * share_rows, share_rows, 0
    )
    ratio_share = measured_share / jnp.sqrt(share + FLOOR_TERM)
    ratios = lax.all_gather(ratio_share, "mode", axis=0, tiled=True)
    factor = (ratios - 1.0)[None, None] * weights[None, :, None, None]
    diff_real = field_real * factor
    diff_imag = field_imag * factor
    ret_real, ret_imag = spectral_updates(
        diff_real, diff_imag, pupil_real, pupil_imag, offsets, wide_cols, size_k
    )
    for source_index in range(source_count):
        start_col = offsets[source_index, 1]
        spec_real = add_window(spec_real, ret_real[:, source_index], start_col, length)
        spec_imag = add_window(spec_imag, ret_imag[:, source_index], start_col, length)
    return (spec_real, spec_imag)


RADIX = 4
ROW_TILE = 64


def split_pair(table):
    high = table.astype(ml_dtypes.bfloat16)
    low = (table - high.astype(np.float64)).astype(ml_dtypes.bfloat16)
    return np.stack([high, low])


def radix_tables(length):
    part = length // RADIX
    t = np.arange(RADIX)[:, None, None]
    r = np.arange(part)[None, :, None]
    s = np.arange(part)[None, None, :]
    angles = (r * (t + RADIX * s) % length) * (2.0 * np.pi / length)
    cos_t = np.cos(angles) / np.sqrt(length)
    sin_t = np.sin(angles) / np.sqrt(length)
    swap = lambda x: np.swapaxes(x, 1, 2)
    width = part // RADIX
    pieces = lambda x: x.reshape(RADIX, part, RADIX, width)
    beside = lambda x, y: np.stack([pieces(x), pieces(y)], axis=3).reshape(RADIX, part, 2 * part)
    columns = np.concatenate([beside(cos_t, sin_t), beside(-sin_t, cos_t)], axis=1)
    rows = np.concatenate([swap(cos_t), swap(sin_t)], axis=1)
    rows_back = np.concatenate([cos_t, sin_t], axis=1)
    return tuple(split_pair(table) for table in (columns, rows, rows_back))


def halves(x):
    high = x.astype(jnp.bfloat16)
    low = (x - high.astype(jnp.float32)).astype(jnp.bfloat16)
    return high, low


def dot(a, b):
    return jnp.dot(a, b, preferred_element_type=jnp.float32)


def dot_right(pair_ref, table_ref, t, turned=False):
    def product(a, b):
        dims = (((1,), (1 if turned else 0,)), ((), ()))
        return lax.dot_general(a, b, dims, preferred_element_type=jnp.float32)

    high, low = pair_ref[0], pair_ref[1]
    return (
        product(high, table_ref[0, t])
        + product(low, table_ref[0, t])
        + product(high, table_ref[1, t])
    )


def dot_left(table_ref, t, high, low):
    return dot(table_ref[0, t], high) + dot(table_ref[0, t], low) + dot(table_ref[1, t], high)


def over_rows(rows, step):
    def one(i, _):
        step(pl.ds(pl.multiple_of(i * ROW_TILE, ROW_TILE), ROW_TILE))
        return 0

    lax.fori_loop(0, rows // ROW_TILE, one, 0)


def lanes_of(x, slots):
    width = x.shape[1] // slots
    return [x[:, n * width : (n + 1) * width] for n in range(slots)]


def times_i(x):
    half = x.shape[1] // 2
    turned = pltpu.roll(x, half, 1)
    return jnp.where(lax.broadcasted_iota(jnp.int32, x.shape, 1) < half, -turned, turned)


def lit_offsets(params_ref, leds, nth):
    row, col, seen = jnp.int32(0), jnp.int32(0), jnp.int32(0)
    for led in range(leds):
        lit = params_ref[led] != 0
        take = jnp.logical_and(lit, seen == nth)
        row = jnp.where(take, params_ref[leds + 2 * led], row)
        col = jnp.where(take, params_ref[leds + 2 * led + 1], col)
        seen = seen + lit.astype(jnp.int32)
    return row, col


def place_of(params_ref, leds, levels=False):
    return params_ref[3 * leds + (1 if levels else 0)]


def pupil_send_kernel(leds, params_ref, real_ref, imag_ref, out_ref):
    length = real_ref.shape[1]
    part = length // RADIX
    for nth in range(out_ref.shape[1]):
        row, _ = lit_offsets(params_ref, leds, nth)
        for index, ref in enumerate((real_ref, imag_ref)):
            rolled = pltpu.roll(ref[...], lax.rem(row, length), 1)
            for q in range(RADIX):
                block = rolled[:, q * part : (q + 1) * part].T
                out_ref[q, nth, index] = block
                out_ref[q + RADIX, nth, index] = block


def window_pupil(leds, params_ref, stage_ref, pupil_ref):
    here = place_of(params_ref, leds)
    blocks, count, _, rows, width = stage_ref.shape
    length = blocks * width
    upper, first = here // RADIX, lax.rem(here, RADIX) * rows
    for nth in range(count):
        row, col = lit_offsets(params_ref, leds, nth)

        def tile(at):
            position = first + at.start + lax.broadcasted_iota(jnp.int32, (ROW_TILE, length), 0)
            owned = (position < row).astype(jnp.int32) == upper
            for index in range(2):
                whole = [stage_ref[d, nth, index, at] for d in range(blocks)]
                whole = pltpu.roll(jnp.concatenate(whole, axis=1), lax.rem(col, length), 1)
                pupil_ref[nth, index, at] = jnp.where(owned, whole, 0.0)

        over_rows(rows, tile)


def columns_kernel(leds, chunk, params_ref, real_ref, imag_ref, table_ref, *refs):
    pair_ref = refs[-1]
    if chunk == 0:
        stage_ref, amplitude_ref, out_ref, pupil_ref = refs[:-1]

        @pl.when(pl.program_id(0) == 0)
        def _():
            window_pupil(leds, params_ref, stage_ref, pupil_ref)
    else:
        pupil_ref, out_ref = refs[0], refs[-2]
    rows, size_k = real_ref.shape[1:]
    length = size_k // 2
    for nth in range(out_ref.shape[1]):
        _, col = lit_offsets(params_ref, leds, nth)

        def tile(at):
            wrapped = lax.broadcasted_iota(jnp.int32, (ROW_TILE, length), 1) < col
            p_r, p_i = pupil_ref[nth, 0, at], pupil_ref[nth, 1, at]
            w_r = jnp.where(wrapped, real_ref[0, at, length:], real_ref[0, at, :length])
            w_i = jnp.where(wrapped, imag_ref[0, at, length:], imag_ref[0, at, :length])
            x_r = lanes_of(p_r * w_r - p_i * w_i, RADIX)
            x_i = lanes_of(p_r * w_i + p_i * w_r, RADIX)
            sum_r, sum_i = x_r[0] + x_r[2], x_i[0] + x_i[2]
            dif_r, dif_i = x_r[0] - x_r[2], x_i[0] - x_i[2]
            odd_r, odd_i = x_r[1] + x_r[3], x_i[1] + x_i[3]
            rot_r, rot_i = x_i[3] - x_i[1], x_r[1] - x_r[3]
            if chunk == 0:
                pairs = ((sum_r + odd_r, sum_i + odd_i), (dif_r + rot_r, dif_i + rot_i))
            else:
                pairs = ((sum_r - odd_r, sum_i - odd_i), (dif_r - rot_r, dif_i - rot_i))
            for t, pair in enumerate(pairs):
                pair_ref[t, 0, at], pair_ref[t, 1, at] = halves(jnp.concatenate(pair, axis=1))

        over_rows(rows, tile)
        for t in range(2):
            z = dot_right(pair_ref[t], table_ref, t)
            for u, piece in enumerate(lanes_of(z, RADIX)):
                out_ref[RADIX * t + u, nth, 0, :rows] = piece
    if chunk == 0:
        out_ref[:, :, 0, rows:] = amplitude_ref[:, :, 0]


def rows_kernel(leds, waits, params_ref, table_ref, got_ref, *refs):
    total_ref, pair_ref = refs[-2:]
    groups, count, modes, _, width = got_ref.shape
    levels = total_ref.shape[0]
    refs = refs[waits:-2]
    field_ref, total_refs = refs[0], refs[1 : 1 + levels]
    part = field_ref.shape[1]
    for amplitude_ref in refs[1 + levels :]:
        amplitude_ref[...] = got_ref[:, :, :, part:]
    slots = [(nth, mode) for nth in range(count) for mode in range(modes)]

    def tile(at):
        for n, (nth, mode) in enumerate(slots):
            x = [got_ref[q, nth, mode, at] + got_ref[q + RADIX, nth, mode, at] for q in range(RADIX)]
            even, odd = x[0] + x[2], x[1] + x[3]
            dif, rot = x[0] - x[2], times_i(x[1] - x[3])
            for t, value in enumerate((even + odd, dif + rot, even - odd, dif - rot)):
                lanes = slice(n * width, (n + 1) * width)
                pair_ref[t, 0, at, lanes], pair_ref[t, 1, at, lanes] = halves(value)

    over_rows(part, tile)
    powers = []
    for t in range(RADIX):
        both = dot_left(table_ref, t, pair_ref[t, 0], pair_ref[t, 1])
        power = None
        for n, (a, b) in enumerate(
            zip(lanes_of(both[:part], len(slots)), lanes_of(both[part:], len(slots)))
        ):
            z = a + times_i(b)
            field_ref[t, :, n * width : (n + 1) * width] = z
            power = z * z if power is None else power + z * z
        powers.append(power + pltpu.roll(power, width // 2, 1))
    rows = total_ref.shape[2] // 2
    low = lax.broadcasted_iota(jnp.int32, (part, width), 1) < width // 2
    for pair in range(2):
        packed = jnp.where(low, powers[2 * pair], powers[2 * pair + 1])
        for d in range(groups):
            for z in range(levels):
                first = (d * levels + z) * rows
                total_ref[z, d, pair * rows : (pair + 1) * rows] = packed[first : first + rows]
    level = place_of(params_ref, leds, True)
    for k, ref in enumerate(total_refs):
        ref[...] = total_ref[lax.rem(level + k, levels)]


def rows_back_kernel(leds, params_ref, table_ref, field_ref, *refs):
    out_ref, factor_ref, turn_ref = refs[-3:]
    groups, count, modes, part, width = out_ref.shape
    levels = factor_ref.shape[0]
    level = place_of(params_ref, leds, True)
    for k, ref in enumerate(refs[:levels]):
        factor_ref[lax.rem(level + levels - k, levels)] = ref[...]
    slots = [(nth, mode) for nth in range(count) for mode in range(modes)]
    rows = factor_ref.shape[2] // 2
    low = lax.broadcasted_iota(jnp.int32, (part, width), 1) < width // 2
    for t in range(RADIX):
        pair = t // 2
        packed = jnp.concatenate(
            [
                factor_ref[z, d, pair * rows : (pair + 1) * rows]
                for d in range(groups)
                for z in range(levels)
            ],
            axis=0,
        )
        turned = pltpu.roll(packed, width // 2, 1)
        factor = jnp.where(low, packed, turned) if t % 2 == 0 else jnp.where(low, turned, packed)
        diff = jnp.concatenate([x * factor for x in lanes_of(field_ref[t], len(slots))], axis=1)
        both = dot_left(table_ref, t, *halves(diff))
        for n, (a, b) in enumerate(
            zip(lanes_of(both[:part], len(slots)), lanes_of(both[part:], len(slots)))
        ):
            turn_ref[t, :, n * width : (n + 1) * width] = a - times_i(b)

    def tile(at):
        for n, (nth, mode) in enumerate(slots):
            v = [turn_ref[t, at, n * width : (n + 1) * width] for t in range(RADIX)]
            even, odd = v[0] + v[2], v[1] + v[3]
            dif, rot = v[0] - v[2], times_i(v[1] - v[3])
            for q, value in enumerate((even + odd, dif - rot, even - odd, dif + rot)):
                out_ref[q, nth, mode, at] = value
                out_ref[q + RADIX, nth, mode, at] = value

    over_rows(part, tile)


def columns_back_kernel(leds, chunk, params_ref, real_ref, imag_ref, table_ref, *refs):
    got_ref, pupil_ref, _, out_r, out_i, pair_ref, turn_ref = refs
    count = got_ref.shape[1]
    rows, size_k = real_ref.shape[1:]
    length = size_k // 2
    for nth in range(count):
        for t in range(2):

            def split(at):
                z = [got_ref[RADIX * t + n, nth, 0, at] for n in range(RADIX)]
                pair_ref[t, 0, at], pair_ref[t, 1, at] = halves(jnp.concatenate(z, axis=1))

            over_rows(rows, split)
            turn_ref[nth, t] = dot_right(pair_ref[t], table_ref, t, True)

    def tile(at):
        totals = [[ref[0, at, :length], ref[0, at, length:]] for ref in (real_ref, imag_ref)]
        for nth in range(count):
            _, col = lit_offsets(params_ref, leds, nth)
            wrapped = lax.broadcasted_iota(jnp.int32, (ROW_TILE, length), 1) < col
            p_r, p_i = pupil_ref[nth, 0, at], pupil_ref[nth, 1, at]
            (a_r, a_i), (b_r, b_i) = [lanes_of(turn_ref[nth, t, at], 2) for t in range(2)]
            if chunk == 0:
                x_r = [a_r + b_r, a_r + b_i, a_r - b_r, a_r - b_i]
                x_i = [a_i + b_i, a_i - b_r, a_i - b_i, a_i + b_r]
            else:
                x_r = [a_r + b_r, -a_r - b_i, a_r - b_r, b_i - a_r]
                x_i = [a_i + b_i, b_r - a_i, a_i - b_i, -a_i - b_r]
            x_r, x_i = jnp.concatenate(x_r, axis=1), jnp.concatenate(x_i, axis=1)
            for total, delta in zip(totals, (p_r * x_r + p_i * x_i, p_r * x_i - p_i * x_r)):
                total[0] = total[0] + jnp.where(wrapped, 0.0, delta)
                total[1] = total[1] + jnp.where(wrapped, delta, 0.0)
        for out, total in zip((out_r, out_i), totals):
            out[0, at, :length] = total[0]
            out[0, at, length:] = total[1]

    over_rows(rows, tile)


SMEM_SPEC = pl.BlockSpec(memory_space=pltpu.SMEM)
ANY_SPEC = pl.BlockSpec(memory_space=pl.ANY)


def room(count):
    return pltpu.CompilerParams(vmem_limit_bytes=(16 + 16 * count) * 1024 * 1024)


CHUNKS = 2


def fixed(shape):
    zeros = (0,) * len(shape)
    return pl.BlockSpec(shape, lambda *_: zeros)


def one_mode(shape):
    before = len(shape) - 3
    block = shape[:before] + (1,) + shape[before + 1 :]
    return pl.BlockSpec(block, lambda i: (0,) * before + (i, 0, 0))


def kept(shape):
    zeros = (0,) * len(shape)
    return pl.BlockSpec(shape, lambda *_: zeros, pipeline_mode=pl.Buffered(1))


def cost(macs, *arrays):
    moved = sum(math.prod(a.shape) * a.dtype.itemsize for a in arrays)
    return pl.CostEstimate(flops=2 * macs, bytes_accessed=moved, transcendentals=0)


def shaped(shape):
    return jax.ShapeDtypeStruct(shape, jnp.float32)


def exchange(blocks):
    return lax.all_to_all(blocks, "rows", split_axis=0, concat_axis=0, tiled=True)


def around(levels, value_of):
    ring = range(levels)
    return [value_of(0)] + [
        lax.ppermute(value_of(k), "mode", [(z, (z + k) % levels) for z in ring]) for k in ring[1:]
    ]


def amplitude_kernel(leds, params_ref, measured_ref, out_ref):
    groups, rows, lanes = out_ref.shape
    width, length = measured_ref.shape[1:]
    columns = lanes // 2
    depth = rows // RADIX
    first = place_of(params_ref, leds, True) * rows

    def pick(x, y, turned):
        total = None
        for _ in range(3):
            x_part = x.astype(jnp.bfloat16)
            x = x - x_part.astype(jnp.float32)
            piece = dot(y, x_part) if turned else dot(x_part, y)
            total = piece if total is None else total + piece
        return total

    def ones_where(condition):
        return jnp.where(condition, 1.0, 0.0).astype(jnp.bfloat16)

    order = lax.broadcasted_iota(jnp.int32, (rows, width), 0)
    source = RADIX * (order % depth) + 2 * ((order // depth) % 2) + order // (2 * depth)
    taken = lax.broadcasted_iota(jnp.int32, (rows, width), 1) == source + first
    mine = pick(measured_ref[0], ones_where(taken), True)
    part = length // RADIX
    from_col = lax.broadcasted_iota(jnp.int32, (length, part), 0)
    to_col = lax.broadcasted_iota(jnp.int32, (length, part), 1)
    half = rows // 2
    for t in range(RADIX):
        chunk, side = t // 2, t % 2
        found = pick(mine, ones_where(from_col == RADIX * to_col + t), False)
        for u, piece in enumerate(lanes_of(found, RADIX)):
            out_ref[RADIX * side + u, chunk * half : (chunk + 1) * half] = jnp.concatenate(
                [piece[:half], piece[half:]], axis=1
            )


def fast_body(object_real, object_imag, pupil_real, pupil_imag, measured, source_mask, offsets):
    width, length = pupil_real.shape
    modes, local_rows, size_k = object_real.shape
    groups, levels = lax.axis_size("rows"), lax.axis_size("mode")
    part = length // RADIX
    leds = offsets.shape[0]
    tables = [jnp.asarray(table) for table in radix_tables(length)]
    position = jnp.stack([lax.axis_index("rows"), lax.axis_index("mode")]).astype(jnp.int32)
    params = jnp.concatenate([source_mask.reshape(-1), offsets.reshape(-1), position])
    spectrum = pl.BlockSpec((1, local_rows, size_k), lambda i: (i, 0, 0))

    def update(count):
        slots = count * modes
        dft_macs = 3 * slots * 2 * 4 * part * part * local_rows
        pupil_shape = (groups, count, 2, local_rows, width)
        block_shape = (groups, count, modes, local_rows, width)
        half_table = (2, RADIX // CHUNKS) + tables[0].shape[2:]

        def columns(chunk, pupil, others):
            extra = others.shape[1] // slots if chunk == 0 else 0
            out = shaped(block_shape[:3] + (local_rows + extra, width))
            whole = shaped((count, 2, local_rows, length))
            specs = [
                SMEM_SPEC,
                spectrum,
                spectrum,
                pl.BlockSpec(half_table, lambda i: (0, chunk, 0, 0), pipeline_mode=pl.Buffered(1)),
            ]
            outs, out_specs = (out,), (one_mode(out.shape),)
            if chunk == 0:
                others = others.reshape(groups, count, modes, extra, width)
                specs += [kept(pupil_shape), one_mode(others.shape)]
                outs, out_specs = outs + (whole,), out_specs + (fixed(whole.shape),)
            else:
                specs += [kept(whole.shape), ANY_SPEC]
            sent, *kept_pupil = pl.pallas_call(
                functools.partial(columns_kernel, leds, chunk),
                out_shape=outs,
                grid=(modes,),
                in_specs=specs,
                out_specs=out_specs,
                scratch_shapes=[pltpu.VMEM((2, 2, local_rows, 2 * part), jnp.bfloat16)],
                compiler_params=room(count),
                cost_estimate=cost(dft_macs, out, out, object_real, object_imag),
                name="columns",
            )(params, object_real, object_imag, tables[0], pupil, others)
            return exchange(sent), kept_pupil, sent

        def rows(got, waits):
            field = shaped((RADIX, part, slots * width))
            total = shaped((groups, 2 * part // groups // levels, width))
            extra = got.shape[3] - local_rows
            outs = (field,) + (total,) * levels
            if extra > 0:
                outs += (shaped((groups, count, modes, extra, width)),)
            return pl.pallas_call(
                functools.partial(rows_kernel, leds, len(waits)),
                out_shape=outs,
                grid=(1,),
                in_specs=[SMEM_SPEC, fixed(tables[1].shape)]
                + [fixed(got.shape)]
                + [ANY_SPEC] * len(waits),
                out_specs=tuple(fixed(out.shape) for out in outs),
                scratch_shapes=[
                    pltpu.VMEM((levels,) + total.shape, jnp.float32),
                    pltpu.VMEM((RADIX, 2, part, slots * width), jnp.bfloat16),
                ],
                compiler_params=room(count),
                cost_estimate=cost(dft_macs, got, field),
                name="rows",
            )(params, tables[1], got, *waits)

        def rows_back(field, factor):
            out = shaped(block_shape)
            sent = pl.pallas_call(
                functools.partial(rows_back_kernel, leds),
                out_shape=out,
                grid=(1,),
                in_specs=[SMEM_SPEC, fixed(tables[2].shape), fixed(field.shape)]
                + [fixed(factor[0].shape)] * levels,
                out_specs=fixed(block_shape),
                scratch_shapes=[
                    pltpu.VMEM((levels,) + factor[0].shape, jnp.float32),
                    pltpu.VMEM(field.shape, jnp.float32),
                ],
                compiler_params=room(count),
                cost_estimate=cost(dft_macs, out, field),
                name="rows_back",
            )(params, tables[2], field, *factor)
            return exchange(sent), sent

        def columns_back(chunk, pupil, got, current, wait):
            out = shaped(object_real.shape)
            return pl.pallas_call(
                functools.partial(columns_back_kernel, leds, chunk),
                out_shape=(out, out),
                grid=(modes,),
                in_specs=[
                    SMEM_SPEC,
                    spectrum,
                    spectrum,
                    pl.BlockSpec(
                        half_table, lambda i: (0, chunk, 0, 0), pipeline_mode=pl.Buffered(1)
                    ),
                    one_mode(block_shape),
                    kept(pupil.shape),
                    ANY_SPEC,
                ],
                out_specs=(spectrum, spectrum),
                scratch_shapes=[
                    pltpu.VMEM((2, 2, local_rows, 2 * part), jnp.bfloat16),
                    pltpu.VMEM((count, 2, local_rows, 2 * part), jnp.float32),
                ],
                input_output_aliases={1: 0, 2: 1} if chunk > 0 else {},
                compiler_params=room(count),
                cost_estimate=cost(dft_macs, got, pupil, out, out, out, out),
                name="columns_back",
            )(params, *current, tables[0], got, pupil, wait)

        def run(*_):
            amplitude = shaped((groups, width // levels, width))
            amplitude = pl.pallas_call(
                functools.partial(amplitude_kernel, leds),
                out_shape=amplitude,
                grid=(1,),
                in_specs=[SMEM_SPEC, fixed(measured.shape)],
                out_specs=fixed(amplitude.shape),
                compiler_params=room(count),
                cost_estimate=cost(3 * length * length * RADIX * 8, amplitude, measured),
                name="amplitude",
            )(params, measured)
            out = shaped(pupil_shape)
            sent = pl.pallas_call(
                functools.partial(pupil_send_kernel, leds),
                out_shape=out,
                grid=(1,),
                in_specs=[SMEM_SPEC] + [fixed(pupil_real.shape)] * 2,
                out_specs=fixed(pupil_shape),
                compiler_params=room(count),
                cost_estimate=cost(0, out, pupil_real, pupil_imag),
                name="pupil_send",
            )(params, pupil_real, pupil_imag)
            got, (pupil,), wait = columns(0, exchange(sent), amplitude)
            more, _, wait = columns(1, pupil, wait)
            got = [got, more]
            back, waits = [], [wait]
            for chunk in range(CHUNKS):
                field, *totals = rows(got[chunk], waits)
                if chunk == 0:
                    mine = totals.pop().reshape(groups, width // levels, width)
                share = sum(around(levels, lambda k: totals[k]))
                deep = share.shape[1]
                ratio = mine[:, chunk * deep : (chunk + 1) * deep] / jnp.sqrt(share + FLOOR_TERM)
                factor = around(levels, lambda k: ratio - 1.0)
                blocks, wait = rows_back(field, factor)
                back.append(blocks)
                waits = [wait]
            current = (object_real, object_imag)
            for chunk in range(CHUNKS):
                current = columns_back(chunk, pupil, back[chunk], current, wait)
            return tuple(current)

        return run

    lit = jnp.sum((source_mask[0] != 0).astype(jnp.int32))
    most = max(leds - 1, 1)
    if most == 1:
        return update(1)()
    return lax.switch(jnp.clip(lit - 1, 0, most - 1), [update(n + 1) for n in range(most)])


def fits_fast(mesh, object_shape, pupil_shape, leds):
    groups, levels = mesh.shape["rows"], mesh.shape["mode"]
    length, size_k = pupil_shape[1], object_shape[2]
    modes, local_rows, width = object_shape[0] // levels, size_k // groups, length // groups
    amplitude_rows = width // levels
    return (
        size_k == 2 * length
        and groups == 2 * RADIX
        and levels == RADIX
        and local_rows % 256 == 0
        and width % 128 == 0
        and all(amplitude_rows % (8 * modes * n) == 0 for n in range(1, max(leds, 2)))
    )


def solution(mesh):
    in_specs = (
        P("mode", "rows", None),
        P("mode", "rows", None),
        P("rows", None),
        P("rows", None),
        P(None, "rows", None),
        P(),
        P(),
    )
    out_specs = (P("mode", "rows", None), P("mode", "rows", None))

    def chosen(object_real, object_imag, pupil_real, *others):
        fast = fits_fast(mesh, object_real.shape, pupil_real.shape, others[-1].shape[0])
        mapped = jax.shard_map(
            fast_body if fast else body,
            mesh=mesh,
            in_specs=in_specs,
            out_specs=out_specs,
            check_vma=False,
        )
        return mapped(object_real, object_imag, pupil_real, *others)

    return chosen
```

profile of v0, /device:TPU:0, one launch (start us, length us, event | category | flops | bytes accessed | tf_op | source)
XLA Modules:
  0.0 311.6 jit_solution(10756554598892747956)
XLA Ops:
  4.2 307.4 %conditional.1 = ((f32[2,256,2048]{2,1,0:T(8,128)}, f32[2,256,2048]{2,1,0:T(8,128)})) conditional(s32[]{:T(128)} %clamp.3, (s32[11]{0:T(128)S(1)}, f32[128,1024]{1,0:T(8,128)}, f32[128,1024]{1,0:T(8,128)}, f32[1,128,1024]{2,1,0:T(8,128)}, f32[2,256,2048]{2,1,0:T(8,128)}, /*index=5*/f32[2,256,2048]{2,1,0:T(8,128)}, (), (), ()) %tuple.13, ...), branch_computations={%region_1.2_spmd, %region_2.3_spmd} | conditional | flops 25971326976 | bytes 293733152 | solution.py:715
  8.8 5.3 %all-to-all-start.5 = ((f32[8,2,2,256,128]{4,3,2,1,0:T(8,128)}), f32[8,2,2,256,128]{4,3,2,1,0:T(8,128)}, u32[]{:S(2)}, u32[]{:S(2)}) async-start(f32[8,2,2,256,128]{4,3,2,1,0:T(8,128)} %copy-done.7), calls=%async_computation.5 | async-start | bytes 8388608 | tf_op jit(solution)/shard_map/cond/branch_1_fun/all_to_all | solution.py:501
  16.3 47.0 %all-to-all-done.5.refs_0_ = f32[8,2,2,256,128]{4,3,2,1,0:T(8,128)} async-done(((f32[8,2,2,256,128]{4,3,2,1,0:T(8,128)}), f32[8,2,2,256,128]{4,3,2,1,0:T(8,128)}, u32[]{:S(2)}, u32[]{:S(2)}) %all-to-all-start.5) | async-done | bytes 4194336 | tf_op jit(solution)/shard_map/cond/branch_1_fun/all_to_all | solution.py:501
  63.4 13.5 %columns.6 = (f32[8,2,2,264,128]{4,3,2,1,0:T(8,128)}, f32[2,2,256,1024]{3,2,1,0:T(8,128)S(1)}) custom-call(s32[11]{0:T(128)S(1)} %get-tuple-element.60.params_ref, f32[2,256,2048]{2,1,0:T(8,128)} %get-tuple-element.115.real_ref, f32[2,256,2048]{2,1,0:T(8,128)} %get-tuple-element.117.imag_ref, bf16[2,4,512,512]{3,2,1,0:T(8,128)(2,1)} %constant.33.clone.2.table_ref, ...), custom_call_target="tpu_custom_call" | custom-call | flops 3221225472 | bytes 17039360 | tf_op jit(solution)/shard_map/cond/branch_1_fun/columns/pallas_call | solution.py:582
  79.0 4.6 %all-to-all-start.6 = ((f32[8,2,2,264,128]{4,3,2,1,0:T(8,128)}), f32[8,2,2,264,128]{4,3,2,1,0:T(8,128)}, u32[]{:S(2)}, u32[]{:S(2)}) async-start(f32[8,2,2,264,128]{4,3,2,1,0:T(8,128)} %get-tuple-element.69.refs_1_), calls=%async_computation.6 | async-start | bytes 8650752 | tf_op jit(solution)/shard_map/cond/branch_1_fun/all_to_all | solution.py:501
  83.6 10.6 %columns.7.refs_0_ = f32[8,2,2,256,128]{4,3,2,1,0:T(8,128)S(1)} custom-call(s32[11]{0:T(128)S(1)} %get-tuple-element.60.params_ref, f32[2,256,2048]{2,1,0:T(8,128)} %get-tuple-element.115.real_ref, f32[2,256,2048]{2,1,0:T(8,128)} %get-tuple-element.117.imag_ref, bf16[2,4,512,512]{3,2,1,0:T(8,128)(2,1)} %constant.33.clone.2.table_ref, ...), custom_call_target="tpu_custom_call" | custom-call | flops 3221225472 | bytes 16777216 | tf_op jit(solution)/shard_map/cond/branch_1_fun/columns/pallas_call | solution.py:582
  96.2 37.9 %all-to-all-done.6.got_ref = f32[8,2,2,264,128]{4,3,2,1,0:T(8,128)} async-done(((f32[8,2,2,264,128]{4,3,2,1,0:T(8,128)}), f32[8,2,2,264,128]{4,3,2,1,0:T(8,128)}, u32[]{:S(2)}, u32[]{:S(2)}) %all-to-all-start.6) | async-done | bytes 4325408 | tf_op jit(solution)/shard_map/cond/branch_1_fun/all_to_all | solution.py:501
  134.1 4.6 %all-to-all-start.8 = ((f32[8,2,2,256,128]{4,3,2,1,0:T(8,128)}), f32[8,2,2,256,128]{4,3,2,1,0:T(8,128)}, u32[]{:S(2)}, u32[]{:S(2)}) async-start(f32[8,2,2,256,128]{4,3,2,1,0:T(8,128)} %copy-done.8), calls=%async_computation.8 | async-start | bytes 8388608 | tf_op jit(solution)/shard_map/cond/branch_1_fun/all_to_all | solution.py:501
  140.3 5.0 %rows.6 = (f32[4,256,512]{2,1,0:T(8,128)S(1)}, f32[8,16,128]{2,1,0:T(8,128)S(1)}, f32[8,16,128]{2,1,0:T(8,128)S(1)}, f32[8,16,128]{2,1,0:T(8,128)S(1)}, f32[8,16...) custom-call(s32[11]{0:T(128)S(1)} %get-tuple-element.60.params_ref, bf16[2,4,512,256]{3,2,1,0:T(8,128)(2,1)S(1)} %copy-done.20, ...), custom_call_target="tpu_custom_call" | custom-call | flops 3221225472 | bytes 6422528 | tf_op jit(solution)/shard_map/cond/branch_1_fun/rows/pallas_call | solution.py:602
  152.6 2.7 collective-permute-done.13
  155.6 2.7 collective-permute-start.17
  160.8 4.3 %collective-permute-done.16.refs_2_ = f32[8,16,128]{2,1,0:T(8,128)S(1)} collective-permute-done((f32[8,16,128]{2,1,0:T(8,128)S(1)}, f32[8,16,128]{2,1,0:T(8,128)S(1)}, u32[]{:S(2)}, u32[]{:S(2)}) %collective-permute-start.16) | collective-permute-done | bytes 65568 | tf_op jit(solution)/shard_map/cond/branch_1_fun/ppermute | solution.py:507
  165.2 5.1 %rows_back.6.refs_0_ = f32[8,2,2,256,128]{4,3,2,1,0:T(8,128)} custom-call(s32[11]{0:T(128)S(1)} %get-tuple-element.60.params_ref, bf16[2,4,512,256]{3,2,1,0:T(8,128)(2,1)S(1)} %copy-done.19, f32[4,256,512]{2,1,0:T(8,128)S(1)} %get-tuple-element.71.field_ref, f32[8,16,128]{2,1,0:T(8,128)S(1)} %fusion.3.refs_0_, ...), custom_call_target="tpu_custom_call" | custom-call | flops 3221225472 | bytes 6291456 | tf_op jit(solution)/shard_map/cond/branch_1_fun/rows_back/pallas_call | solution.py:621
  170.3 17.5 %all-to-all-done.8.got_ref = f32[8,2,2,256,128]{4,3,2,1,0:T(8,128)} async-done(((f32[8,2,2,256,128]{4,3,2,1,0:T(8,128)}), f32[8,2,2,256,128]{4,3,2,1,0:T(8,128)}, u32[]{:S(2)}, u32[]{:S(2)}) %all-to-all-start.8) | async-done | bytes 4194336 | tf_op jit(solution)/shard_map/cond/branch_1_fun/all_to_all | solution.py:501
  187.8 4.8 %all-to-all-start.7 = ((f32[8,2,2,256,128]{4,3,2,1,0:T(8,128)}), f32[8,2,2,256,128]{4,3,2,1,0:T(8,128)}, u32[]{:S(2)}, u32[]{:S(2)}) async-start(f32[8,2,2,256,128]{4,3,2,1,0:T(8,128)} %rows_back.6.refs_0_), calls=%async_computation.7 | async-start | bytes 8388608 | tf_op jit(solution)/shard_map/cond/branch_1_fun/all_to_all | solution.py:501
  194.2 4.8 %rows.7 = (f32[4,256,512]{2,1,0:T(8,128)S(1)}, f32[8,16,128]{2,1,0:T(8,128)S(1)}, f32[8,16,128]{2,1,0:T(8,128)S(1)}, f32[8,16,128]{2,1,0:T(8,128)S(1)}, f32[8,16,128]{2,1,0:T(8,128)S(1)}) custom-call(s32[11]{0:T(128)S(1)} %get-tuple-element.60.params_ref, bf16[2,4,512,256]{3,2,1,0:T(8,128)(2,1)S(1)} %copy-done.21, ...), custom_call_target="tpu_custom_call" | custom-call | flops 3221225472 | bytes 6291456 | tf_op jit(solution)/shard_map/cond/branch_1_fun/rows/pallas_call | solution.py:602
  209.1 2.9 collective-permute-start.23
  214.3 4.4 %collective-permute-done.22.refs_2_ = f32[8,16,128]{2,1,0:T(8,128)S(1)} collective-permute-done((f32[8,16,128]{2,1,0:T(8,128)S(1)}, f32[8,16,128]{2,1,0:T(8,128)S(1)}, u32[]{:S(2)}, u32[]{:S(2)}) %collective-permute-start.22) | collective-permute-done | bytes 65568 | tf_op jit(solution)/shard_map/cond/branch_1_fun/ppermute | solution.py:507
  218.7 5.1 %rows_back.7.refs_2_ = f32[8,2,2,256,128]{4,3,2,1,0:T(8,128)} custom-call(s32[11]{0:T(128)S(1)} %get-tuple-element.60.params_ref, bf16[2,4,512,256]{3,2,1,0:T(8,128)(2,1)S(1)} %copy-done.19, f32[4,256,512]{2,1,0:T(8,128)S(1)} %get-tuple-element.77.field_ref, f32[8,16,128]{2,1,0:T(8,128)S(1)} %fusion.2.refs_0_, ...), custom_call_target="tpu_custom_call" | custom-call | flops 3221225472 | bytes 6291456 | tf_op jit(solution)/shard_map/cond/branch_1_fun/rows_back/pallas_call | solution.py:621
  223.8 17.7 %all-to-all-done.7.refs_0_ = f32[8,2,2,256,128]{4,3,2,1,0:T(8,128)} async-done(((f32[8,2,2,256,128]{4,3,2,1,0:T(8,128)}), f32[8,2,2,256,128]{4,3,2,1,0:T(8,128)}, u32[]{:S(2)}, u32[]{:S(2)}) %all-to-all-start.7) | async-done | bytes 4194336 | tf_op jit(solution)/shard_map/cond/branch_1_fun/all_to_all | solution.py:501
  241.5 4.6 %all-to-all-start.9 = ((f32[8,2,2,256,128]{4,3,2,1,0:T(8,128)}), f32[8,2,2,256,128]{4,3,2,1,0:T(8,128)}, u32[]{:S(2)}, u32[]{:S(2)}) async-start(f32[8,2,2,256,128]{4,3,2,1,0:T(8,128)} %rows_back.7.refs_2_), calls=%async_computation.9 | async-start | bytes 8388608 | tf_op jit(solution)/shard_map/cond/branch_1_fun/all_to_all | solution.py:501
  248.3 14.1 %columns_back.6 = (f32[2,256,2048]{2,1,0:T(8,128)}, f32[2,256,2048]{2,1,0:T(8,128)}) custom-call(s32[11]{0:T(128)S(1)} %get-tuple-element.60.params_ref, f32[2,256,2048]{2,1,0:T(8,128)} %get-tuple-element.115.real_ref, f32[2,256,2048]{2,1,0:T(8,128)} %get-tuple-element.117.imag_ref, bf16[2,4,512,512]{3,2,1,0:T(8,128)(2,1)S(1)} %copy-done, ...), custom_call_target="tpu_custom_call" | custom-call | flops 3221225472 | bytes 25165824 | tf_op jit(solution)/shard_map/cond/branch_1_fun/columns_back/pallas_call | solution.py:640
  262.4 32.8 %all-to-all-done.9.refs_0_ = f32[8,2,2,256,128]{4,3,2,1,0:T(8,128)} async-done(((f32[8,2,2,256,128]{4,3,2,1,0:T(8,128)}), f32[8,2,2,256,128]{4,3,2,1,0:T(8,128)}, u32[]{:S(2)}, u32[]{:S(2)}) %all-to-all-start.9) | async-done | bytes 4194336 | tf_op jit(solution)/shard_map/cond/branch_1_fun/all_to_all | solution.py:501
  297.4 14.2 %columns_back.7 = (f32[2,256,2048]{2,1,0:T(8,128)}, f32[2,256,2048]{2,1,0:T(8,128)}) custom-call(s32[11]{0:T(128)S(1)} %get-tuple-element.60.params_ref, f32[2,256,2048]{2,1,0:T(8,128)} %get-tuple-element.82.real_ref, f32[2,256,2048]{2,1,0:T(8,128)} %get-tuple-element.83.imag_ref, ...), custom_call_target="tpu_custom_call", output_to_operand_aliasing={{0}: (1, {}), {1}: (2, {})} | custom-call | flops 3221225472 | bytes 25165824 | tf_op jit(solution)/shard_map/cond/branch_1_fun/columns_back/pallas_call | solution.py:640
  (45 shorter events, 43.6 us)
Async XLA Ops:
  6.8 2.0 copy-start.7
  8.8 5.3 %copy-start.23 = (f32[1,128,1024]{2,1,0:T(8,128)S(1)}, f32[1,128,1024]{2,1,0:T(8,128)}, u32[]{:S(2)}) copy-start(f32[1,128,1024]{2,1,0:T(8,128)} %get-tuple-element.113.measured_ref) | copy-start | bytes 1572868 | tf_op jit(solution)/shard_map/cond
  8.8 54.5 %all-to-all-start.5 = ((f32[8,2,2,256,128]{4,3,2,1,0:T(8,128)}), f32[8,2,2,256,128]{4,3,2,1,0:T(8,128)}, u32[]{:S(2)}, u32[]{:S(2)}) async-start(f32[8,2,2,256,128]{4,3,2,1,0:T(8,128)} %copy-done.7), calls=%async_computation.5 | async-start | bytes 8388608 | tf_op jit(solution)/shard_map/cond/branch_1_fun/all_to_all | solution.py:501
  76.9 2.1 copy-start.6
  79.0 55.1 %all-to-all-start.6 = ((f32[8,2,2,264,128]{4,3,2,1,0:T(8,128)}), f32[8,2,2,264,128]{4,3,2,1,0:T(8,128)}, u32[]{:S(2)}, u32[]{:S(2)}) async-start(f32[8,2,2,264,128]{4,3,2,1,0:T(8,128)} %get-tuple-element.69.refs_1_), calls=%async_computation.6 | async-start | bytes 8650752 | tf_op jit(solution)/shard_map/cond/branch_1_fun/all_to_all | solution.py:501
  94.2 2.0 copy-start.8
  134.1 53.7 %all-to-all-start.8 = ((f32[8,2,2,256,128]{4,3,2,1,0:T(8,128)}), f32[8,2,2,256,128]{4,3,2,1,0:T(8,128)}, u32[]{:S(2)}, u32[]{:S(2)}) async-start(f32[8,2,2,256,128]{4,3,2,1,0:T(8,128)} %copy-done.8), calls=%async_computation.8 | async-start | bytes 8388608 | tf_op jit(solution)/shard_map/cond/branch_1_fun/all_to_all | solution.py:501
  140.3 24.9 %copy-start.19 = (bf16[2,4,512,256]{3,2,1,0:T(8,128)(2,1)S(1)}, bf16[2,4,512,256]{3,2,1,0:T(8,128)(2,1)}, u32[]{:S(2)}) copy-start(bf16[2,4,512,256]{3,2,1,0:T(8,128)(2,1)} %constant.35.clone.2.table_ref) | copy-start | bytes 6291460 | tf_op jit(solution)/shard_map/cond
  145.3 7.2 %collective-permute-start.12 = (f32[8,16,128]{2,1,0:T(8,128)S(1)}, f32[8,16,128]{2,1,0:T(8,128)S(1)}, u32[]{:S(2)}, u32[]{:S(2)}) collective-permute-start(f32[8,16,128]{2,1,0:T(8,128)S(1)} %get-tuple-element.74), channel_id=1, source_target_pairs={{0,8},{8,16},{16,24},{24,0},{1,9},{9,17},{17,25},{25,1},{2,10},{10... | collective-permute-start | bytes 196616 | tf_op jit(solution)/shard_map/cond/branch_1_fun/ppermute | solution.py:507
  147.8 7.5 %collective-permute-start.13 = (f32[8,16,128]{2,1,0:T(8,128)S(1)}, f32[8,16,128]{2,1,0:T(8,128)S(1)}, u32[]{:S(2)}, u32[]{:S(2)}) collective-permute-start(f32[8,16,128]{2,1,0:T(8,128)S(1)} %get-tuple-element.75), channel_id=1, source_target_pairs={{0,16},{8,24},{16,0},{24,8},{1,17},{9,25},{17,1},{25,9},{2,18},{10... | collective-permute-start | bytes 196616 | tf_op jit(solution)/shard_map/cond/branch_1_fun/ppermute | solution.py:507
  150.4 5.2 %collective-permute-start.14 = (f32[8,16,128]{2,1,0:T(8,128)S(1)}, f32[8,16,128]{2,1,0:T(8,128)S(1)}, u32[]{:S(2)}, u32[]{:S(2)}) collective-permute-start(f32[8,16,128]{2,1,0:T(8,128)S(1)} %get-tuple-element.76), channel_id=1, source_target_pairs={{0,24},{8,0},{16,8},{24,16},{1,25},{9,1},{17,9},{25,17},{2,26},{10... | collective-permute-start | bytes 196616 | tf_op jit(solution)/shard_map/cond/branch_1_fun/ppermute | solution.py:507
  155.6 5.2 %collective-permute-start.17 = (f32[8,16,128]{2,1,0:T(8,128)S(1)}, f32[8,16,128]{2,1,0:T(8,128)S(1)}, u32[]{:S(2)}, u32[]{:S(2)}) collective-permute-start(f32[8,16,128]{2,1,0:T(8,128)S(1)} %fusion.3.refs_0_), channel_id=1, source_target_pairs={{0,24},{8,0},{16,8},{24,16},{1,25},{9,1},{17,9},{25,17},{2,26},{10... | collective-permute-start | bytes 196616 | tf_op jit(solution)/shard_map/cond/branch_1_fun/ppermute | solution.py:507
  158.3 6.9 %collective-permute-start.16 = (f32[8,16,128]{2,1,0:T(8,128)S(1)}, f32[8,16,128]{2,1,0:T(8,128)S(1)}, u32[]{:S(2)}, u32[]{:S(2)}) collective-permute-start(f32[8,16,128]{2,1,0:T(8,128)S(1)} %fusion.3.refs_0_), channel_id=1, source_target_pairs={{0,16},{8,24},{16,0},{24,8},{1,17},{9,25},{17,1},{25,9},{2,18},{10... | collective-permute-start | bytes 196616 | tf_op jit(solution)/shard_map/cond/branch_1_fun/ppermute | solution.py:507
  158.7 6.5 %collective-permute-start.15 = (f32[8,16,128]{2,1,0:T(8,128)S(1)}, f32[8,16,128]{2,1,0:T(8,128)S(1)}, u32[]{:S(2)}, u32[]{:S(2)}) collective-permute-start(f32[8,16,128]{2,1,0:T(8,128)S(1)} %fusion.3.refs_0_), channel_id=1, source_target_pairs={{0,8},{8,16},{16,24},{24,0},{1,9},{9,17},{17,25},{25,1},{2,10},{10... | collective-permute-start | bytes 196616 | tf_op jit(solution)/shard_map/cond/branch_1_fun/ppermute | solution.py:507
  187.8 53.7 %all-to-all-start.7 = ((f32[8,2,2,256,128]{4,3,2,1,0:T(8,128)}), f32[8,2,2,256,128]{4,3,2,1,0:T(8,128)}, u32[]{:S(2)}, u32[]{:S(2)}) async-start(f32[8,2,2,256,128]{4,3,2,1,0:T(8,128)} %rows_back.6.refs_0_), calls=%async_computation.7 | async-start | bytes 8388608 | tf_op jit(solution)/shard_map/cond/branch_1_fun/all_to_all | solution.py:501
  199.1 7.0 %collective-permute-start.18 = (f32[8,16,128]{2,1,0:T(8,128)S(1)}, f32[8,16,128]{2,1,0:T(8,128)S(1)}, u32[]{:S(2)}, u32[]{:S(2)}) collective-permute-start(f32[8,16,128]{2,1,0:T(8,128)S(1)} %get-tuple-element.79), channel_id=1, source_target_pairs={{0,8},{8,16},{16,24},{24,0},{1,9},{9,17},{17,25},{25,1},{2,10},{10... | collective-permute-start | bytes 196616 | tf_op jit(solution)/shard_map/cond/branch_1_fun/ppermute | solution.py:507
  201.5 7.3 %collective-permute-start.19 = (f32[8,16,128]{2,1,0:T(8,128)S(1)}, f32[8,16,128]{2,1,0:T(8,128)S(1)}, u32[]{:S(2)}, u32[]{:S(2)}) collective-permute-start(f32[8,16,128]{2,1,0:T(8,128)S(1)} %get-tuple-element.80), channel_id=1, source_target_pairs={{0,16},{8,24},{16,0},{24,8},{1,17},{9,25},{17,1},{25,9},{2,18},{10... | collective-permute-start | bytes 196616 | tf_op jit(solution)/shard_map/cond/branch_1_fun/ppermute | solution.py:507
  204.1 5.0 %collective-permute-start.20 = (f32[8,16,128]{2,1,0:T(8,128)S(1)}, f32[8,16,128]{2,1,0:T(8,128)S(1)}, u32[]{:S(2)}, u32[]{:S(2)}) collective-permute-start(f32[8,16,128]{2,1,0:T(8,128)S(1)} %get-tuple-element.81), channel_id=1, source_target_pairs={{0,24},{8,0},{16,8},{24,16},{1,25},{9,1},{17,9},{25,17},{2,26},{10... | collective-permute-start | bytes 196616 | tf_op jit(solution)/shard_map/cond/branch_1_fun/ppermute | solution.py:507
  209.1 5.2 %collective-permute-start.23 = (f32[8,16,128]{2,1,0:T(8,128)S(1)}, f32[8,16,128]{2,1,0:T(8,128)S(1)}, u32[]{:S(2)}, u32[]{:S(2)}) collective-permute-start(f32[8,16,128]{2,1,0:T(8,128)S(1)} %fusion.2.refs_0_), channel_id=1, source_target_pairs={{0,24},{8,0},{16,8},{24,16},{1,25},{9,1},{17,9},{25,17},{2,26},{10... | collective-permute-start | bytes 196616 | tf_op jit(solution)/shard_map/cond/branch_1_fun/ppermute | solution.py:507
  212.0 6.7 %collective-permute-start.22 = (f32[8,16,128]{2,1,0:T(8,128)S(1)}, f32[8,16,128]{2,1,0:T(8,128)S(1)}, u32[]{:S(2)}, u32[]{:S(2)}) collective-permute-start(f32[8,16,128]{2,1,0:T(8,128)S(1)} %fusion.2.refs_0_), channel_id=1, source_target_pairs={{0,16},{8,24},{16,0},{24,8},{1,17},{9,25},{17,1},{25,9},{2,18},{10... | collective-permute-start | bytes 196616 | tf_op jit(solution)/shard_map/cond/branch_1_fun/ppermute | solution.py:507
  212.2 6.5 %collective-permute-start.21 = (f32[8,16,128]{2,1,0:T(8,128)S(1)}, f32[8,16,128]{2,1,0:T(8,128)S(1)}, u32[]{:S(2)}, u32[]{:S(2)}) collective-permute-start(f32[8,16,128]{2,1,0:T(8,128)S(1)} %fusion.2.refs_0_), channel_id=1, source_target_pairs={{0,8},{8,16},{16,24},{24,0},{1,9},{9,17},{17,25},{25,1},{2,10},{10... | collective-permute-start | bytes 196616 | tf_op jit(solution)/shard_map/cond/branch_1_fun/ppermute | solution.py:507
  241.5 53.7 %all-to-all-start.9 = ((f32[8,2,2,256,128]{4,3,2,1,0:T(8,128)}), f32[8,2,2,256,128]{4,3,2,1,0:T(8,128)}, u32[]{:S(2)}, u32[]{:S(2)}) async-start(f32[8,2,2,256,128]{4,3,2,1,0:T(8,128)} %rows_back.7.refs_2_), calls=%async_computation.9 | async-start | bytes 8388608 | tf_op jit(solution)/shard_map/cond/branch_1_fun/all_to_all | solution.py:501
  246.1 2.2 copy-start
  295.2 2.2 copy-start.1
  (2 other events, 3.2 us)
where the time goes:
time: 312 us
  waiting for transfers between devices  173 us (55%)
  Pallas kernels  77.2 us (25%)
  starting transfers between devices  43.4 us (14%)
  local copies, waits for them, and re-layouts  14.5 us (5%)
    all_to_all x5, waiting for transfers between devices, exchange(): lax.all_to_all(blocks, 'rows', split_axis=0, concat_axis=0, tiled=True)  153 us
    pallas_call x2, Pallas kernels, columns_back(): pl.pallas_call(functools.partial(columns_back_kernel, leds, chunk), out_s...  28.3 us
    pallas_call x2, Pallas kernels, columns(): pl.pallas_call(functools.partial(columns_kernel, leds, chunk), out_shape=...  24.1 us
    all_to_all x5, starting transfers between devices, exchange(): lax.all_to_all(blocks, 'rows', split_axis=0, concat_axis=0, tiled=True)  23.8 us
    ppermute x12, waiting for transfers between devices, around(): lax.ppermute(value_of(k), 'mode', [(z, (z + k) % levels) for z in ring])  19.8 us
    ppermute x12, starting transfers between devices, around(): lax.ppermute(value_of(k), 'mode', [(z, (z + k) % levels) for z in ring])  19.6 us
    cond x18, local copies, waits for them, and re-layouts  13.7 us
    pallas_call x2, Pallas kernels, rows_back(): pl.pallas_call(functools.partial(rows_back_kernel, leds), out_shape=out,...  10.2 us
  transfers between devices with their start and end apart: 17, of which 15 were waited for; matrix products, arithmetic and copies ran while one was open for 0% of the time, Pallas kernels for 15%

commit v1 on v0

--- a/solution.py
+++ b/solution.py
@@ -174,7 +174,7 @@
 
 
 RADIX = 4
-ROW_TILE = 64
+ROW_TILE = 16
 
 
 def split_pair(table):
@@ -233,7 +233,7 @@
         step(pl.ds(pl.multiple_of(i * ROW_TILE, ROW_TILE), ROW_TILE))
         return 0
 
-    lax.fori_loop(0, rows // ROW_TILE, one, 0)
+    lax.fori_loop(0, rows // ROW_TILE, one, 0, unroll=2)
 
 
 def lanes_of(x, slots):
@@ -462,7 +462,7 @@
 
 
 SMEM_SPEC = pl.BlockSpec(memory_space=pltpu.SMEM)
-ANY_SPEC = pl.BlockSpec(memory_space=pl.ANY)
+ANY_SPEC = pl.BlockSpec(memory_space=pltpu.HBM)
 
 
 def room(count):
@@ -497,8 +497,13 @@
     return jax.ShapeDtypeStruct(shape, jnp.float32)
 
 
+def in_hbm(shape):
+    return pltpu.HBM(shape, jnp.float32)
+
+
 def exchange(blocks):
-    return lax.all_to_all(blocks, "rows", split_axis=0, concat_axis=0, tiled=True)
+    got = lax.all_to_all(blocks, "rows", split_axis=0, concat_axis=0, tiled=True)
+    return pltpu.with_memory_space_constraint(got, pltpu.HBM)
 
 
 def around(levels, value_of):
@@ -564,7 +569,7 @@
 
         def columns(chunk, pupil, others):
             extra = others.shape[1] // slots if chunk == 0 else 0
-            out = shaped(block_shape[:3] + (local_rows + extra, width))
+            out = in_hbm(block_shape[:3] + (local_rows + extra, width))
             whole = shaped((count, 2, local_rows, length))
             specs = [
                 SMEM_SPEC,
@@ -590,7 +595,7 @@
                 cost_estimate=cost(dft_macs, out, out, object_real, object_imag),
                 name="columns",
             )(params, object_real, object_imag, tables[0], pupil, others)
-            return exchange(sent), kept_pupil, sent
+            return exchange(sent), kept_pupil, pltpu.with_memory_space_constraint(sent, pltpu.HBM)
 
         def rows(got, waits):
             field = shaped((RADIX, part, slots * width))
@@ -617,7 +622,7 @@
             )(params, tables[1], got, *waits)
 
         def rows_back(field, factor):
-            out = shaped(block_shape)
+            out = in_hbm(block_shape)
             sent = pl.pallas_call(
                 functools.partial(rows_back_kernel, leds),
                 out_shape=out,
@@ -633,7 +638,7 @@
                 cost_estimate=cost(dft_macs, out, field),
                 name="rows_back",
             )(params, tables[2], field, *factor)
-            return exchange(sent), sent
+            return exchange(sent), pltpu.with_memory_space_constraint(sent, pltpu.HBM)
 
         def columns_back(chunk, pupil, got, current, wait):
             out = shaped(object_real.shape)
@@ -675,7 +680,7 @@
                 cost_estimate=cost(3 * length * length * RADIX * 8, amplitude, measured),
                 name="amplitude",
             )(params, measured)
-            out = shaped(pupil_shape)
+            out = in_hbm(pupil_shape)
             sent = pl.pallas_call(
                 functools.partial(pupil_send_kernel, leds),
                 out_shape=out,

time: 312 us -> 314 us (level)
  Pallas kernels: 77.2 us -> 82.6 us
    cond x18 -> x16, local copies, waits for them, and re-layouts: 13.7 us -> 11.8 us
  transfers between devices with their start and end apart: 17 -> 17, of which waited for: 15 -> 15; matrix products, arithmetic and copies ran while one was open for 0% -> 0% of each run, Pallas kernels for 15% -> 16%
where the time goes in v1:
time: 314 us; the launch traced here: 313 us
  waiting for transfers between devices  170 us (54%)
  Pallas kernels  82.6 us (26%)
  starting transfers between devices  43.4 us (14%)
  local copies, waits for them, and re-layouts  12.7 us (4%)
    all_to_all x5, waiting for transfers between devices, exchange(): lax.all_to_all(blocks, 'rows', split_axis=0, concat_axis=0, tiled=True)  151 us
    pallas_call x2, Pallas kernels, columns_back(): pl.pallas_call(functools.partial(columns_back_kernel, leds, chunk), out_s...  29 us
    pallas_call x2, Pallas kernels, columns(): pl.pallas_call(functools.partial(columns_kernel, leds, chunk), out_shape=...  25.7 us
    all_to_all x5, starting transfers between devices, exchange(): lax.all_to_all(blocks, 'rows', split_axis=0, concat_axis=0, tiled=True)  23.8 us
    ppermute x12, waiting for transfers between devices, around(): lax.ppermute(value_of(k), 'mode', [(z, (z + k) % levels) for z in ring])  19.8 us
    ppermute x12, starting transfers between devices, around(): lax.ppermute(value_of(k), 'mode', [(z, (z + k) % levels) for z in ring])  19.6 us
    cond x16, local copies, waits for them, and re-layouts  11.8 us
    pallas_call x2, Pallas kernels, rows_back(): pl.pallas_call(functools.partial(rows_back_kernel, leds), out_shape=out,...  10.8 us
  transfers between devices with their start and end apart: 17, of which 15 were waited for; matrix products, arithmetic and copies ran while one was open for 0% of the time, Pallas kernels for 16%

profile of v1, /device:TPU:0, one launch (start us, length us, event | category | flops | bytes accessed | tf_op | source)
XLA Modules:
  0.0 312.7 jit_solution(15611924143148475410)
XLA Ops:
  4.2 308.6 %conditional.1 = ((f32[2,256,2048]{2,1,0:T(8,128)}, f32[2,256,2048]{2,1,0:T(8,128)})) conditional(s32[]{:T(128)} %clamp.3, (s32[11]{0:T(128)S(1)}, f32[128,1024]{1,0:T(8,128)}, f32[128,1024]{1,0:T(8,128)}, f32[1,128,1024]{2,1,0:T(8,128)}, f32[2,256,2048]{2,1,0:T(8,128)}, /*index=5*/f32[2,256,2048]{2,1,0:T(8,128)}, (), (), ()) %tuple.13, ...), branch_computations={%region_1.2_spmd, %region_2.3_spmd} | conditional | flops 25971326976 | bytes 276955904 | solution.py:720
  4.3 4.5 %pupil_send.3 = f32[8,2,2,256,128]{4,3,2,1,0:T(8,128)} custom-call(s32[11]{0:T(128)S(1)} %get-tuple-element.60.params_ref, f32[128,1024]{1,0:T(8,128)} %get-tuple-element.109.real_ref, f32[128,1024]{1,0:T(8,128)} %get-tuple-element.111.imag_ref), custom_call_target="tpu_custom_call" | custom-call | bytes 5242880 | tf_op jit(solution)/shard_map/cond/branch_1_fun/pupil_send/pallas_call | solution.py:684
  8.8 5.3 %all-to-all-start.5 = ((f32[8,2,2,256,128]{4,3,2,1,0:T(8,128)}), f32[8,2,2,256,128]{4,3,2,1,0:T(8,128)}, u32[]{:S(2)}, u32[]{:S(2)}) async-start(f32[8,2,2,256,128]{4,3,2,1,0:T(8,128)} %pupil_send.3), calls=%async_computation.5 | async-start | bytes 8388608 | tf_op jit(solution)/shard_map/cond/branch_1_fun/all_to_all | solution.py:505
  16.3 47.0 %all-to-all-done.5.refs_0_ = f32[8,2,2,256,128]{4,3,2,1,0:T(8,128)} async-done(((f32[8,2,2,256,128]{4,3,2,1,0:T(8,128)}), f32[8,2,2,256,128]{4,3,2,1,0:T(8,128)}, u32[]{:S(2)}, u32[]{:S(2)}) %all-to-all-start.5) | async-done | bytes 4194336 | tf_op jit(solution)/shard_map/cond/branch_1_fun/all_to_all | solution.py:505
  63.4 14.3 %columns.6 = (f32[8,2,2,264,128]{4,3,2,1,0:T(8,128)}, f32[2,2,256,1024]{3,2,1,0:T(8,128)S(1)}) custom-call(s32[11]{0:T(128)S(1)} %get-tuple-element.60.params_ref, f32[2,256,2048]{2,1,0:T(8,128)} %get-tuple-element.115.real_ref, f32[2,256,2048]{2,1,0:T(8,128)} %get-tuple-element.117.imag_ref, bf16[2,4,512,512]{3,2,1,0:T(8,128)(2,1)} %constant.33.clone.2.table_ref, ...), custom_call_target="tpu_custom_call" | custom-call | flops 3221225472 | bytes 17039360 | tf_op jit(solution)/shard_map/cond/branch_1_fun/columns/pallas_call | solution.py:587
  79.8 4.6 %all-to-all-start.6 = ((f32[8,2,2,264,128]{4,3,2,1,0:T(8,128)}), f32[8,2,2,264,128]{4,3,2,1,0:T(8,128)}, u32[]{:S(2)}, u32[]{:S(2)}) async-start(f32[8,2,2,264,128]{4,3,2,1,0:T(8,128)} %get-tuple-element.69.refs_1_), calls=%async_computation.6 | async-start | bytes 8650752 | tf_op jit(solution)/shard_map/cond/branch_1_fun/all_to_all | solution.py:505
  86.6 11.3 %columns.7.refs_0_ = f32[8,2,2,256,128]{4,3,2,1,0:T(8,128)} custom-call(s32[11]{0:T(128)S(1)} %get-tuple-element.60.params_ref, f32[2,256,2048]{2,1,0:T(8,128)} %get-tuple-element.115.real_ref, f32[2,256,2048]{2,1,0:T(8,128)} %get-tuple-element.117.imag_ref, bf16[2,4,512,512]{3,2,1,0:T(8,128)(2,1)S(1)} %copy-done, f32[2,2,256,1024]{3,2,1,0:T(8,128)} %copy-done.7, ...), custom_call_target="tpu_custom_call" | custom-call | flops 3221225472 | bytes 16777216 | tf_op jit(solution)/shard_map/cond/branch_1_fun/columns/pallas_call | solution.py:587
  97.9 37.0 %all-to-all-done.6.got_ref = f32[8,2,2,264,128]{4,3,2,1,0:T(8,128)} async-done(((f32[8,2,2,264,128]{4,3,2,1,0:T(8,128)}), f32[8,2,2,264,128]{4,3,2,1,0:T(8,128)}, u32[]{:S(2)}, u32[]{:S(2)}) %all-to-all-start.6) | async-done | bytes 4325408 | tf_op jit(solution)/shard_map/cond/branch_1_fun/all_to_all | solution.py:505
  134.9 4.6 %all-to-all-start.8 = ((f32[8,2,2,256,128]{4,3,2,1,0:T(8,128)}), f32[8,2,2,256,128]{4,3,2,1,0:T(8,128)}, u32[]{:S(2)}, u32[]{:S(2)}) async-start(f32[8,2,2,256,128]{4,3,2,1,0:T(8,128)} %columns.7.refs_0_), calls=%async_computation.8 | async-start | bytes 8388608 | tf_op jit(solution)/shard_map/cond/branch_1_fun/all_to_all | solution.py:505
  141.1 5.3 %rows.6 = (f32[4,256,512]{2,1,0:T(8,128)S(1)}, f32[8,16,128]{2,1,0:T(8,128)S(1)}, f32[8,16,128]{2,1,0:T(8,128)S(1)}, f32[8,16,128]{2,1,0:T(8,128)S(1)}, f32[8,16...) custom-call(s32[11]{0:T(128)S(1)} %get-tuple-element.60.params_ref, bf16[2,4,512,256]{3,2,1,0:T(8,128)(2,1)S(1)} %copy-done.13, ...), custom_call_target="tpu_custom_call" | custom-call | flops 3221225472 | bytes 6422528 | tf_op jit(solution)/shard_map/cond/branch_1_fun/rows/pallas_call | solution.py:607
  156.7 2.7 collective-permute-start.17
  161.9 4.3 %collective-permute-done.16.refs_2_ = f32[8,16,128]{2,1,0:T(8,128)S(1)} collective-permute-done((f32[8,16,128]{2,1,0:T(8,128)S(1)}, f32[8,16,128]{2,1,0:T(8,128)S(1)}, u32[]{:S(2)}, u32[]{:S(2)}) %collective-permute-start.16) | collective-permute-done | bytes 65568 | tf_op jit(solution)/shard_map/cond/branch_1_fun/ppermute | solution.py:512
  166.3 5.4 %rows_back.6.refs_0_ = f32[8,2,2,256,128]{4,3,2,1,0:T(8,128)} custom-call(s32[11]{0:T(128)S(1)} %get-tuple-element.60.params_ref, bf16[2,4,512,256]{3,2,1,0:T(8,128)(2,1)S(1)} %copy-done.12, f32[4,256,512]{2,1,0:T(8,128)S(1)} %get-tuple-element.71.field_ref, f32[8,16,128]{2,1,0:T(8,128)S(1)} %fusion.3.refs_0_, ...), custom_call_target="tpu_custom_call" | custom-call | flops 3221225472 | bytes 6291456 | tf_op jit(solution)/shard_map/cond/branch_1_fun/rows_back/pallas_call | solution.py:626
  171.7 16.9 %all-to-all-done.8.got_ref = f32[8,2,2,256,128]{4,3,2,1,0:T(8,128)} async-done(((f32[8,2,2,256,128]{4,3,2,1,0:T(8,128)}), f32[8,2,2,256,128]{4,3,2,1,0:T(8,128)}, u32[]{:S(2)}, u32[]{:S(2)}) %all-to-all-start.8) | async-done | bytes 4194336 | tf_op jit(solution)/shard_map/cond/branch_1_fun/all_to_all | solution.py:505
  188.6 4.8 %all-to-all-start.7 = ((f32[8,2,2,256,128]{4,3,2,1,0:T(8,128)}), f32[8,2,2,256,128]{4,3,2,1,0:T(8,128)}, u32[]{:S(2)}, u32[]{:S(2)}) async-start(f32[8,2,2,256,128]{4,3,2,1,0:T(8,128)} %rows_back.6.refs_0_), calls=%async_computation.7 | async-start | bytes 8388608 | tf_op jit(solution)/shard_map/cond/branch_1_fun/all_to_all | solution.py:505
  195.0 5.1 %rows.7 = (f32[4,256,512]{2,1,0:T(8,128)S(1)}, f32[8,16,128]{2,1,0:T(8,128)S(1)}, f32[8,16,128]{2,1,0:T(8,128)S(1)}, f32[8,16,128]{2,1,0:T(8,128)S(1)}, f32[8,16,128]{2,1,0:T(8,128)S(1)}) custom-call(s32[11]{0:T(128)S(1)} %get-tuple-element.60.params_ref, bf16[2,4,512,256]{3,2,1,0:T(8,128)(2,1)S(1)} %copy-done.14, ...), custom_call_target="tpu_custom_call" | custom-call | flops 3221225472 | bytes 6291456 | tf_op jit(solution)/shard_map/cond/branch_1_fun/rows/pallas_call | solution.py:607
  210.2 2.9 collective-permute-start.23
  215.4 4.4 %collective-permute-done.22.refs_2_ = f32[8,16,128]{2,1,0:T(8,128)S(1)} collective-permute-done((f32[8,16,128]{2,1,0:T(8,128)S(1)}, f32[8,16,128]{2,1,0:T(8,128)S(1)}, u32[]{:S(2)}, u32[]{:S(2)}) %collective-permute-start.22) | collective-permute-done | bytes 65568 | tf_op jit(solution)/shard_map/cond/branch_1_fun/ppermute | solution.py:512
  219.8 5.4 %rows_back.7.refs_2_ = f32[8,2,2,256,128]{4,3,2,1,0:T(8,128)} custom-call(s32[11]{0:T(128)S(1)} %get-tuple-element.60.params_ref, bf16[2,4,512,256]{3,2,1,0:T(8,128)(2,1)S(1)} %copy-done.12, f32[4,256,512]{2,1,0:T(8,128)S(1)} %get-tuple-element.77.field_ref, f32[8,16,128]{2,1,0:T(8,128)S(1)} %fusion.2.refs_0_, ...), custom_call_target="tpu_custom_call" | custom-call | flops 3221225472 | bytes 6291456 | tf_op jit(solution)/shard_map/cond/branch_1_fun/rows_back/pallas_call | solution.py:626
  225.1 17.2 %all-to-all-done.7.refs_0_ = f32[8,2,2,256,128]{4,3,2,1,0:T(8,128)} async-done(((f32[8,2,2,256,128]{4,3,2,1,0:T(8,128)}), f32[8,2,2,256,128]{4,3,2,1,0:T(8,128)}, u32[]{:S(2)}, u32[]{:S(2)}) %all-to-all-start.7) | async-done | bytes 4194336 | tf_op jit(solution)/shard_map/cond/branch_1_fun/all_to_all | solution.py:505
  242.3 4.6 %all-to-all-start.9 = ((f32[8,2,2,256,128]{4,3,2,1,0:T(8,128)}), f32[8,2,2,256,128]{4,3,2,1,0:T(8,128)}, u32[]{:S(2)}, u32[]{:S(2)}) async-start(f32[8,2,2,256,128]{4,3,2,1,0:T(8,128)} %rows_back.7.refs_2_), calls=%async_computation.9 | async-start | bytes 8388608 | tf_op jit(solution)/shard_map/cond/branch_1_fun/all_to_all | solution.py:505
  249.1 14.5 %columns_back.6 = (f32[2,256,2048]{2,1,0:T(8,128)}, f32[2,256,2048]{2,1,0:T(8,128)}) custom-call(s32[11]{0:T(128)S(1)} %get-tuple-element.60.params_ref, f32[2,256,2048]{2,1,0:T(8,128)} %get-tuple-element.115.real_ref, f32[2,256,2048]{2,1,0:T(8,128)} %get-tuple-element.117.imag_ref, bf16[2,4,512,512]{3,2,1,0:T(8,128)(2,1)S(1)} %copy-done.1, ...), custom_call_target="tpu_custom_call" | custom-call | flops 3221225472 | bytes 25165824 | tf_op jit(solution)/shard_map/cond/branch_1_fun/columns_back/pallas_call | solution.py:645
  263.6 32.5 %all-to-all-done.9.refs_0_ = f32[8,2,2,256,128]{4,3,2,1,0:T(8,128)} async-done(((f32[8,2,2,256,128]{4,3,2,1,0:T(8,128)}), f32[8,2,2,256,128]{4,3,2,1,0:T(8,128)}, u32[]{:S(2)}, u32[]{:S(2)}) %all-to-all-start.9) | async-done | bytes 4194336 | tf_op jit(solution)/shard_map/cond/branch_1_fun/all_to_all | solution.py:505
  298.2 14.5 %columns_back.7 = (f32[2,256,2048]{2,1,0:T(8,128)}, f32[2,256,2048]{2,1,0:T(8,128)}) custom-call(s32[11]{0:T(128)S(1)} %get-tuple-element.60.params_ref, f32[2,256,2048]{2,1,0:T(8,128)} %get-tuple-element.82.real_ref, f32[2,256,2048]{2,1,0:T(8,128)} %get-tuple-element.83.imag_ref, ...), custom_call_target="tpu_custom_call", output_to_operand_aliasing={{0}: (1, {}), {1}: (2, {})} | custom-call | flops 3221225472 | bytes 25165824 | tf_op jit(solution)/shard_map/cond/branch_1_fun/columns_back/pallas_call | solution.py:645
  (43 shorter events, 42.1 us)
Async XLA Ops:
  8.8 5.3 %copy-start.17 = (f32[1,128,1024]{2,1,0:T(8,128)S(1)}, f32[1,128,1024]{2,1,0:T(8,128)}, u32[]{:S(2)}) copy-start(f32[1,128,1024]{2,1,0:T(8,128)} %get-tuple-element.113.measured_ref) | copy-start | bytes 1572868 | tf_op jit(solution)/shard_map/cond
  8.8 54.5 %all-to-all-start.5 = ((f32[8,2,2,256,128]{4,3,2,1,0:T(8,128)}), f32[8,2,2,256,128]{4,3,2,1,0:T(8,128)}, u32[]{:S(2)}, u32[]{:S(2)}) async-start(f32[8,2,2,256,128]{4,3,2,1,0:T(8,128)} %pupil_send.3), calls=%async_computation.5 | async-start | bytes 8388608 | tf_op jit(solution)/shard_map/cond/branch_1_fun/all_to_all | solution.py:505
  77.7 2.1 copy-start.7
  79.8 55.1 %all-to-all-start.6 = ((f32[8,2,2,264,128]{4,3,2,1,0:T(8,128)}), f32[8,2,2,264,128]{4,3,2,1,0:T(8,128)}, u32[]{:S(2)}, u32[]{:S(2)}) async-start(f32[8,2,2,264,128]{4,3,2,1,0:T(8,128)} %get-tuple-element.69.refs_1_), calls=%async_computation.6 | async-start | bytes 8650752 | tf_op jit(solution)/shard_map/cond/branch_1_fun/all_to_all | solution.py:505
  84.4 2.2 copy-start
  134.9 53.7 %all-to-all-start.8 = ((f32[8,2,2,256,128]{4,3,2,1,0:T(8,128)}), f32[8,2,2,256,128]{4,3,2,1,0:T(8,128)}, u32[]{:S(2)}, u32[]{:S(2)}) async-start(f32[8,2,2,256,128]{4,3,2,1,0:T(8,128)} %columns.7.refs_0_), calls=%async_computation.8 | async-start | bytes 8388608 | tf_op jit(solution)/shard_map/cond/branch_1_fun/all_to_all | solution.py:505
  139.5 1.6 copy-start.13
  141.1 25.2 %copy-start.12 = (bf16[2,4,512,256]{3,2,1,0:T(8,128)(2,1)S(1)}, bf16[2,4,512,256]{3,2,1,0:T(8,128)(2,1)}, u32[]{:S(2)}) copy-start(bf16[2,4,512,256]{3,2,1,0:T(8,128)(2,1)} %constant.35.clone.2.table_ref) | copy-start | bytes 6291460 | tf_op jit(solution)/shard_map/cond
  146.4 7.2 %collective-permute-start.12 = (f32[8,16,128]{2,1,0:T(8,128)S(1)}, f32[8,16,128]{2,1,0:T(8,128)S(1)}, u32[]{:S(2)}, u32[]{:S(2)}) collective-permute-start(f32[8,16,128]{2,1,0:T(8,128)S(1)} %get-tuple-element.74), channel_id=1, source_target_pairs={{0,8},{8,16},{16,24},{24,0},{1,9},{9,17},{17,25},{25,1},{2,10},{10... | collective-permute-start | bytes 196616 | tf_op jit(solution)/shard_map/cond/branch_1_fun/ppermute | solution.py:512
  148.8 7.5 %collective-permute-start.13 = (f32[8,16,128]{2,1,0:T(8,128)S(1)}, f32[8,16,128]{2,1,0:T(8,128)S(1)}, u32[]{:S(2)}, u32[]{:S(2)}) collective-permute-start(f32[8,16,128]{2,1,0:T(8,128)S(1)} %get-tuple-element.75), channel_id=1, source_target_pairs={{0,16},{8,24},{16,0},{24,8},{1,17},{9,25},{17,1},{25,9},{2,18},{10... | collective-permute-start | bytes 196616 | tf_op jit(solution)/shard_map/cond/branch_1_fun/ppermute | solution.py:512
  151.4 5.2 %collective-permute-start.14 = (f32[8,16,128]{2,1,0:T(8,128)S(1)}, f32[8,16,128]{2,1,0:T(8,128)S(1)}, u32[]{:S(2)}, u32[]{:S(2)}) collective-permute-start(f32[8,16,128]{2,1,0:T(8,128)S(1)} %get-tuple-element.76), channel_id=1, source_target_pairs={{0,24},{8,0},{16,8},{24,16},{1,25},{9,1},{17,9},{25,17},{2,26},{10... | collective-permute-start | bytes 196616 | tf_op jit(solution)/shard_map/cond/branch_1_fun/ppermute | solution.py:512
  156.7 5.2 %collective-permute-start.17 = (f32[8,16,128]{2,1,0:T(8,128)S(1)}, f32[8,16,128]{2,1,0:T(8,128)S(1)}, u32[]{:S(2)}, u32[]{:S(2)}) collective-permute-start(f32[8,16,128]{2,1,0:T(8,128)S(1)} %fusion.3.refs_0_), channel_id=1, source_target_pairs={{0,24},{8,0},{16,8},{24,16},{1,25},{9,1},{17,9},{25,17},{2,26},{10... | collective-permute-start | bytes 196616 | tf_op jit(solution)/shard_map/cond/branch_1_fun/ppermute | solution.py:512
  159.4 6.9 %collective-permute-start.16 = (f32[8,16,128]{2,1,0:T(8,128)S(1)}, f32[8,16,128]{2,1,0:T(8,128)S(1)}, u32[]{:S(2)}, u32[]{:S(2)}) collective-permute-start(f32[8,16,128]{2,1,0:T(8,128)S(1)} %fusion.3.refs_0_), channel_id=1, source_target_pairs={{0,16},{8,24},{16,0},{24,8},{1,17},{9,25},{17,1},{25,9},{2,18},{10... | collective-permute-start | bytes 196616 | tf_op jit(solution)/shard_map/cond/branch_1_fun/ppermute | solution.py:512
  159.8 6.5 %collective-permute-start.15 = (f32[8,16,128]{2,1,0:T(8,128)S(1)}, f32[8,16,128]{2,1,0:T(8,128)S(1)}, u32[]{:S(2)}, u32[]{:S(2)}) collective-permute-start(f32[8,16,128]{2,1,0:T(8,128)S(1)} %fusion.3.refs_0_), channel_id=1, source_target_pairs={{0,8},{8,16},{16,24},{24,0},{1,9},{9,17},{17,25},{25,1},{2,10},{10... | collective-permute-start | bytes 196616 | tf_op jit(solution)/shard_map/cond/branch_1_fun/ppermute | solution.py:512
  188.6 53.7 %all-to-all-start.7 = ((f32[8,2,2,256,128]{4,3,2,1,0:T(8,128)}), f32[8,2,2,256,128]{4,3,2,1,0:T(8,128)}, u32[]{:S(2)}, u32[]{:S(2)}) async-start(f32[8,2,2,256,128]{4,3,2,1,0:T(8,128)} %rows_back.6.refs_0_), calls=%async_computation.7 | async-start | bytes 8388608 | tf_op jit(solution)/shard_map/cond/branch_1_fun/all_to_all | solution.py:505
  200.1 7.0 %collective-permute-start.18 = (f32[8,16,128]{2,1,0:T(8,128)S(1)}, f32[8,16,128]{2,1,0:T(8,128)S(1)}, u32[]{:S(2)}, u32[]{:S(2)}) collective-permute-start(f32[8,16,128]{2,1,0:T(8,128)S(1)} %get-tuple-element.79), channel_id=1, source_target_pairs={{0,8},{8,16},{16,24},{24,0},{1,9},{9,17},{17,25},{25,1},{2,10},{10... | collective-permute-start | bytes 196616 | tf_op jit(solution)/shard_map/cond/branch_1_fun/ppermute | solution.py:512
  202.5 7.3 %collective-permute-start.19 = (f32[8,16,128]{2,1,0:T(8,128)S(1)}, f32[8,16,128]{2,1,0:T(8,128)S(1)}, u32[]{:S(2)}, u32[]{:S(2)}) collective-permute-start(f32[8,16,128]{2,1,0:T(8,128)S(1)} %get-tuple-element.80), channel_id=1, source_target_pairs={{0,16},{8,24},{16,0},{24,8},{1,17},{9,25},{17,1},{25,9},{2,18},{10... | collective-permute-start | bytes 196616 | tf_op jit(solution)/shard_map/cond/branch_1_fun/ppermute | solution.py:512
  205.1 5.0 %collective-permute-start.20 = (f32[8,16,128]{2,1,0:T(8,128)S(1)}, f32[8,16,128]{2,1,0:T(8,128)S(1)}, u32[]{:S(2)}, u32[]{:S(2)}) collective-permute-start(f32[8,16,128]{2,1,0:T(8,128)S(1)} %get-tuple-element.81), channel_id=1, source_target_pairs={{0,24},{8,0},{16,8},{24,16},{1,25},{9,1},{17,9},{25,17},{2,26},{10... | collective-permute-start | bytes 196616 | tf_op jit(solution)/shard_map/cond/branch_1_fun/ppermute | solution.py:512
  210.2 5.2 %collective-permute-start.23 = (f32[8,16,128]{2,1,0:T(8,128)S(1)}, f32[8,16,128]{2,1,0:T(8,128)S(1)}, u32[]{:S(2)}, u32[]{:S(2)}) collective-permute-start(f32[8,16,128]{2,1,0:T(8,128)S(1)} %fusion.2.refs_0_), channel_id=1, source_target_pairs={{0,24},{8,0},{16,8},{24,16},{1,25},{9,1},{17,9},{25,17},{2,26},{10... | collective-permute-start | bytes 196616 | tf_op jit(solution)/shard_map/cond/branch_1_fun/ppermute | solution.py:512
  213.0 6.7 %collective-permute-start.22 = (f32[8,16,128]{2,1,0:T(8,128)S(1)}, f32[8,16,128]{2,1,0:T(8,128)S(1)}, u32[]{:S(2)}, u32[]{:S(2)}) collective-permute-start(f32[8,16,128]{2,1,0:T(8,128)S(1)} %fusion.2.refs_0_), channel_id=1, source_target_pairs={{0,16},{8,24},{16,0},{24,8},{1,17},{9,25},{17,1},{25,9},{2,18},{10... | collective-permute-start | bytes 196616 | tf_op jit(solution)/shard_map/cond/branch_1_fun/ppermute | solution.py:512
  213.3 6.5 %collective-permute-start.21 = (f32[8,16,128]{2,1,0:T(8,128)S(1)}, f32[8,16,128]{2,1,0:T(8,128)S(1)}, u32[]{:S(2)}, u32[]{:S(2)}) collective-permute-start(f32[8,16,128]{2,1,0:T(8,128)S(1)} %fusion.2.refs_0_), channel_id=1, source_target_pairs={{0,8},{8,16},{16,24},{24,0},{1,9},{9,17},{17,25},{25,1},{2,10},{10... | collective-permute-start | bytes 196616 | tf_op jit(solution)/shard_map/cond/branch_1_fun/ppermute | solution.py:512
  242.3 53.7 %all-to-all-start.9 = ((f32[8,2,2,256,128]{4,3,2,1,0:T(8,128)}), f32[8,2,2,256,128]{4,3,2,1,0:T(8,128)}, u32[]{:S(2)}, u32[]{:S(2)}) async-start(f32[8,2,2,256,128]{4,3,2,1,0:T(8,128)} %rows_back.7.refs_2_), calls=%async_computation.9 | async-start | bytes 8388608 | tf_op jit(solution)/shard_map/cond/branch_1_fun/all_to_all | solution.py:505
  246.9 2.2 copy-start.1
  296.0 2.2 copy-start.2
  (1 other events, 1.6 us)
